TPU v7x, 32 devices: a whole 2x2x4 slice. The times are simulated.
32 devices in a mesh: ctx: 4 (over y, x), tp: 8 (over z, core).
Axes of the slice: x: 2, y: 2, z: 4, core: 2. Of those that a mesh axis runs over, the one named last changes fastest.
Arguments:
- tokens: bfloat16 [512, 16384], P(None, 'ctx'), may hold values from -4 to 4
- wq: bfloat16 [16384, 16384], P('ctx', 'tp'), may hold values from -0.046875 to 0.046875
- wk: bfloat16 [16384, 1024], P('ctx', 'tp'), may hold values from -0.046875 to 0.046875
- wv: bfloat16 [16384, 1024], P('ctx', 'tp'), may hold values from -0.046875 to 0.046875
- doc_len: int32 [16], replicated, may hold values from 1 to 189, as said below
- doc_shard: int32 [16], replicated, may hold values from 0 to 3, as said below
- doc_slot: int32 [16], replicated, may hold values from 0 to 191, as said below
Outputs:
- attended: bfloat16 [768, 16384], P('ctx', 'tp')
Inputs may be any that keep to these rules, and one draw needn't show every extreme that they name: `doc_len`: documents lie in the packed sequence in index order and their lengths sum to 512; in every draw some document has length 189. `doc_shard`: each shard holds exactly 4 documents whose lengths sum to at most 192; in every draw some shard holds exactly 192 tokens. The documents of one shard take disjoint runs of slots doc_slot to doc_slot + doc_len - 1, filling the slots from 0 without gaps; in every draw some document starts at slot 191.
All inputs are finite; a program needn't handle non-finite values.
Results may differ from a plain program's by a relative error of at most 0.035.
Values may be sent and summed in bfloat16 or wider, within the bound.
A program may use at most 64 MiB of HBM per device.

v0:
```python
import jax
import jax.numpy as jnp
from jax import lax
from jax.sharding import PartitionSpec as P

HEAD_SIZE = 128


rope_base = 500000.0


def partner(shard, axis, apart):
    return lax.ppermute(shard, axis, [(i, i ^ 1 << apart) for i in range(lax.axis_size(axis))])


def slot_layout(doc_len, doc_shard, doc_slot, tokens_total, capacity, slot_total):
    ends = jnp.cumsum(doc_len)
    starts = ends - doc_len
    token_ids = jnp.arange(tokens_total, dtype=jnp.int32)
    inside = (token_ids[:, None] >= starts[None, :]) & (token_ids[:, None] < ends[None, :])
    doc_ids = jnp.arange(doc_len.shape[0], dtype=jnp.int32)
    doc_of = jnp.sum(jnp.where(inside, doc_ids[None, :], 0), axis=1)
    first = jnp.sum(jnp.where(inside, starts[None, :], 0), axis=1)
    anchor = doc_shard * capacity + doc_slot
    base = jnp.sum(jnp.where(inside, anchor[None, :], 0), axis=1)
    position = token_ids - first
    target = base + position
    slot_ids = jnp.arange(slot_total, dtype=jnp.int32)
    source = jnp.zeros((slot_total,), jnp.int32).at[target].set(token_ids)
    filled = jnp.zeros((slot_total,), jnp.int32).at[target].set(1)
    slot_doc = jnp.zeros((slot_total,), jnp.int32).at[target].set(doc_of)
    slot_doc = jnp.where(filled == 1, slot_doc, -1 - slot_ids)
    slot_position_index = jnp.zeros((slot_total,), jnp.int32).at[target].set(position)
    return (source, filled, slot_doc, slot_position_index)


def apply_rotary(values, positions):
    head_dim = values.shape[-1]
    half = head_dim // 2
    freq = jnp.power(
        jnp.float32(rope_base), -jnp.arange(half, dtype=jnp.float32) * (2.0 / head_dim)
    )
    angle = positions.astype(jnp.float32)[:, None] * freq[None, :]
    cosine = jnp.cos(angle)[:, None, :]
    sine = jnp.sin(angle)[:, None, :]
    lower = values[..., :half]
    upper = values[..., half:]
    return jnp.concatenate([lower * cosine - upper * sine, upper * cosine + lower * sine], axis=-1)


def attend(query_matrix, key, value_matrix, slot_doc, slot_position_index):
    scale = query_matrix.shape[-1] ** (-0.5)
    scores = (
        jnp.einsum("qgjd,kgd->gjqk", query_matrix, key, preferred_element_type=jnp.float32) * scale
    )
    allowed = (slot_doc[:, None] == slot_doc[None, :]) & (
        slot_position_index[None, :] <= slot_position_index[:, None]
    )
    scores = jnp.where(allowed[None, None], scores, -jnp.inf)
    peak = jnp.max(scores, axis=-1, keepdims=True)
    expo = jnp.exp(scores - peak)
    total = jnp.sum(expo, axis=-1)
    weights = expo.astype(jnp.bfloat16)
    mixed = jnp.einsum("gjqk,kgd->qgjd", weights, value_matrix, preferred_element_type=jnp.float32)
    result = mixed / jnp.transpose(total, (2, 0, 1))[..., None]
    return result.astype(jnp.bfloat16)


def body(tokens, wq, wk, wv, doc_len, doc_shard, doc_slot):
    shards = lax.axis_size("ctx")
    total_tokens = tokens.shape[0]
    per_shard = total_tokens // shards
    capacity = per_shard + per_shard // 2
    slot_total = capacity * shards
    source, filled, slot_doc, slot_position_index = slot_layout(
        doc_len, doc_shard, doc_slot, total_tokens, capacity, slot_total
    )
    joined = jnp.concatenate([wq, wk, wv], axis=1)
    q_cols = wq.shape[1]
    key_value_columns = wk.shape[1]
    picked = jnp.take(tokens, source, axis=0)
    partial_rows = jnp.dot(picked, joined, preferred_element_type=jnp.float32)
    summed = lax.psum_scatter(
        jnp.where(filled[:, None] == 1, partial_rows, jnp.float32(0.0)).astype(jnp.bfloat16),
        "ctx",
        scatter_dimension=0,
        tiled=True,
    ).astype(jnp.float32)
    shard = lax.axis_index("ctx")
    my_doc = lax.dynamic_slice_in_dim(slot_doc, shard * capacity, capacity)
    my_pos = lax.dynamic_slice_in_dim(slot_position_index, shard * capacity, capacity)
    heads_here = q_cols // HEAD_SIZE
    query_matrix = apply_rotary(
        summed[:, :q_cols].reshape(capacity, heads_here, HEAD_SIZE), my_pos
    ).astype(jnp.bfloat16)
    piece = jnp.stack(
        [summed[:, q_cols : q_cols + key_value_columns], summed[:, q_cols + key_value_columns :]],
        axis=0,
    ).astype(jnp.bfloat16)
    members = HEAD_SIZE // key_value_columns
    member = lax.axis_index("tp") % members
    for bit in range(members.bit_length() - 1):
        other = partner(piece, "tp", bit)
        upper_bit = member // 2**bit % 2
        lower_part = jnp.where(upper_bit == 0, piece, other)
        upper_part = jnp.where(upper_bit == 0, other, piece)
        piece = jnp.concatenate([lower_part, upper_part], axis=2)
    key_unrotated = lax.optimization_barrier(piece[0])
    value_matrix = piece[1]
    key = apply_rotary(key_unrotated.astype(jnp.float32)[:, None, :], my_pos).astype(jnp.bfloat16)
    result = attend(
        query_matrix.reshape(capacity, 1, heads_here, HEAD_SIZE),
        key,
        value_matrix[:, None, :],
        my_doc,
        my_pos,
    )
    return result.reshape(capacity, heads_here * HEAD_SIZE)


def solution(mesh):
    return jax.shard_map(
        body,
        mesh=mesh,
        in_specs=(P(None, "ctx"), P("ctx", "tp"), P("ctx", "tp"), P("ctx", "tp"), P(), P(), P()),
        out_specs=P("ctx", "tp"),
        check_vma=False,
    )
```

profile of v0, /device:TPU:0, one launch (start us, length us, event | category | flops | bytes accessed | tf_op | source)
XLA Modules:
  0.0 120.5 jit_solution(14943793533893937592)
XLA Ops:
  6.5 0.0 reduce-scatter.2.cloned.1.call-start
  6.5 0.7 copy.17
  7.3 0.1 reduce.2
  7.4 0.7 sub.35
  8.1 0.7 multiply_add_fusion
  8.8 0.1 select_reduce_fusion
  8.9 2.4 %scatter_custom_fusion.1 = s32[768]{0:T(1024)S(1)} fusion(s32[512]{0:T(512)S(1)} %bitcast.64, s32[512]{0:T(512)S(1)} %iota.27, s32[]{:T(128)} %constant.14.clone.1), kind=kCustom, calls=%fused_computation.73 | custom fusion | bytes 3076 | tf_op jit(solution)/shard_map/scatter | solution.py:29
  11.4 2.4 %scatter_custom_fusion.2 = s32[768]{0:T(1024)S(1)} fusion(s32[512]{0:T(512)S(1)} %bitcast.65, s32[512]{0:T(512)S(1)} %get-tuple-element.5, s32[]{:T(128)} %constant.14.clone.1), kind=kCustom, calls=%fused_computation.71 | custom fusion | bytes 3076 | tf_op jit(solution)/shard_map/scatter | solution.py:31
  13.8 2.6 %scatter_custom_fusion = s32[768]{0:T(1024)S(1)} fusion(s32[512]{0:T(512)S(1)} %bitcast.66, s32[512]{0:T(512)S(1)} %broadcast.163, s32[]{:T(128)} %constant.14.clone.1), kind=kCustom, calls=%fused_computation.75 | custom fusion | bytes 3076 | tf_op jit(solution)/shard_map/scatter | solution.py:30
  16.5 0.0 copy-start.1
  16.5 0.0 copy-start.2
  16.5 14.8 %gather_fusion = bf16[768,4096]{1,0:T(8,128)(2,1)} fusion(bf16[512,4096]{1,0:T(8,128)(2,1)} %param.7, s32[1024]{0:T(1024)S(1)} %pad_clamp_fusion), kind=kCustom, calls=%fused_computation | custom fusion | bytes 12585984 | tf_op jit(solution)/shard_map/jit(_take)/gather | solution.py:81
  31.4 0.0 copy-done.1
  31.4 0.0 copy-done.2
  31.4 23.6 %select_convert_fusion = bf16[768,2304]{1,0:T(8,128)(2,1)} fusion(bf16[4096,128]{1,0:T(8,128)(2,1)S(1)} %copy-done.1, bf16[4096,128]{1,0:T(8,128)(2,1)S(1)} %copy-done.2, bf16[4096,2048]{1,0:T(8,128)(2,1)} %param.8, bf16[768,4096]{1,0:T(8,128)(2,1)} %gather_fusion, pred[768]{0:T(1024)(128)(4,1)S(1)} %compare_and_fusion.1, ...), kind=kOutput, calls=%fused_computation.11 | convolution fusion | flops 14558822400 | bytes 28706304 | tf_op jit(solution)/shard_map/dot_general | solution.py:82
  55.0 0.0 reduce-scatter.2.cloned.1.call-update
  55.0 2.7 %scatter_custom_fusion.3 = s32[768]{0:T(1024)S(1)} fusion(s32[512]{0:T(512)S(1)} %bitcast.67, s32[512]{0:T(512)S(1)} %iota_subtract_fusion, s32[]{:T(128)} %constant.14.clone.1), kind=kCustom, calls=%fused_computation.69 | custom fusion | bytes 3076 | tf_op jit(solution)/shard_map/scatter | solution.py:33
  57.7 0.1 dynamic_slice.6
  57.8 0.1 fusion.56
  57.8 0.1 compare_and_fusion
  58.0 0.4 multiply_cosine_fusion
  58.4 46.7 %reduce-scatter.2.cloned.1.call-done = bf16[192,2304]{1,0:T(8,128)(2,1)} async-done(((bf16[768,2304]{1,0:T(8,128)(2,1)}), bf16[192,2304]{1,0:T(8,128)(2,1)}) %reduce-scatter.2.cloned.1.call-update) | async-done | bytes 884752 | tf_op jit(solution)/shard_map/reduce_scatter | solution.py:83
  105.1 1.3 %convert_bitcast_fusion = f32[24,8,16,128]{3,1,2,0:T(8,128)S(1)} fusion(bf16[192,2304]{1,0:T(8,128)(2,1)} %reduce-scatter.2.cloned.1.call-done), kind=kLoop, calls=%fused_computation.24 | loop fusion | flops 393216 | bytes 2359296
  106.4 0.3 copy.25
  106.7 0.0 slice-start
  106.7 0.5 fusion.57
  107.2 0.3 slice-done
  107.5 0.5 fusion.41
  107.9 1.0 subtract_convert_fusion
  109.0 0.0 copy-start
  109.0 1.0 fusion.15
  110.0 0.7 fusion.13
  110.7 0.0 copy-done
  110.7 1.3 %fusion.19 = bf16[192,1,16,128]{3,0,2,1:T(8,128)(2,1)S(1)} fusion(f32[192,192,16]{1,0,2:T(8,128)S(1)} %get-tuple-element.21, f32[16,192]{1,0:T(8,128)S(1)} %get-tuple-element.20, pred[192,192]{0,1:T(8,128)(4,1)S(1)} %compare_and_fusion, f32[192,16]{0,1:T(8,128)S(1)} %bitcast.62, bf16[192,2304]{1,0:T(8,128)(2,1)S(1)} %copy-done), kind=kOutput, calls=%fused_computation.23 | convolution fusion | flops 154140672 | bytes 4063232 | tf_op jit(solution)/shard_map/gjqk,kgd->qgjd/dot_general | solution.py:64
  112.1 0.5 copy.21
  112.6 1.1 copy.32
  (11 shorter events, 0.1 us)
Async XLA Ops:
  6.5 98.5 %reduce-scatter.2.cloned.1.call-start = ((), (), s32[]{:S(2)}) async-start(), calls=%async_computation.1 | async-start | bytes 4423680 | tf_op jit(solution)/shard_map/reduce_scatter | solution.py:83
  16.5 14.9 %copy-start.1 = (bf16[4096,128]{1,0:T(8,128)(2,1)S(1)}, bf16[4096,128]{1,0:T(8,128)(2,1)}, u32[]{:S(2)}) copy-start(bf16[4096,128]{1,0:T(8,128)(2,1)} %param.10) | copy-start | bytes 3145732
  16.5 14.9 %copy-start.2 = (bf16[4096,128]{1,0:T(8,128)(2,1)S(1)}, bf16[4096,128]{1,0:T(8,128)(2,1)}, u32[]{:S(2)}) copy-start(bf16[4096,128]{1,0:T(8,128)(2,1)} %param.9) | copy-start | bytes 3145732
  106.7 0.8 slice-start
  109.0 1.8 %copy-start = (bf16[192,2304]{1,0:T(8,128)(2,1)S(1)}, bf16[192,2304]{1,0:T(8,128)(2,1)}, u32[]{:S(2)}) copy-start(bf16[192,2304]{1,0:T(8,128)(2,1)} %reduce-scatter.2.cloned.1.call-done) | copy-start | bytes 2654212
Sparse Core Ops, SparseCore 0:
  55.1 49.9 reduce-scatter.1
where the time goes:
time: 121 us
  waiting for transfers between devices  46.7 us (39%)
  local copies, waits for them, and re-layouts  28.5 us (24%)
  matrix products  26 us (21%)
  between operations  13.6 us (11%)
  other arithmetic  5.74 us (5%)
    reduce_scatter x1, waiting for transfers between devices, body(): lax.psum_scatter(jnp.where(filled[:, None] == 1, partial_rows, jnp.float3...  46.7 us
    dot_general x1, matrix products, body(): partial_rows = jnp.dot(picked, joined, preferred_element_type=jnp.float32)  23.6 us
    gather x1, local copies, waits for them, and re-layouts, body(): picked = jnp.take(tokens, source, axis=0)  14.8 us
    scatter x1, local copies, waits for them, and re-layouts, slot_layout(): jnp.zeros((slot_total,), jnp.int32).at[target].set(position)  2.67 us
    scatter x1, local copies, waits for them, and re-layouts, slot_layout(): filled = jnp.zeros((slot_total,), jnp.int32).at[target].set(1)  2.63 us
    scatter x1, local copies, waits for them, and re-layouts, slot_layout(): source = jnp.zeros((slot_total,), jnp.int32).at[target].set(token_ids)  2.45 us
    scatter x1, local copies, waits for them, and re-layouts, slot_layout(): slot_doc = jnp.zeros((slot_total,), jnp.int32).at[target].set(doc_of)  2.45 us
  transfers between devices with their start and end apart: 1, of which 1 were waited for; matrix products, arithmetic and copies ran while one was open for 3% of the time, Pallas kernels for 0%

commit v1 on v0

--- a/solution.py
+++ b/solution.py
@@ -1,6 +1,11 @@
+import functools
+
 import jax
 import jax.numpy as jnp
+import numpy as np
 from jax import lax
+from jax.experimental import pallas as pl
+from jax.experimental.pallas import tpu as pltpu
 from jax.sharding import PartitionSpec as P
 
 HEAD_SIZE = 128
@@ -66,7 +71,7 @@
     return result.astype(jnp.bfloat16)
 
 
-def body(tokens, wq, wk, wv, doc_len, doc_shard, doc_slot):
+def plain(tokens, wq, wk, wv, doc_len, doc_shard, doc_slot):
     shards = lax.axis_size("ctx")
     total_tokens = tokens.shape[0]
     per_shard = total_tokens // shards
@@ -118,6 +123,286 @@
     return result.reshape(capacity, heads_here * HEAD_SIZE)
 
 
+def fused_kernel(
+    shards, capacity, heads_here,
+    len_ref, shard_ref, slot_ref, freq_ref, tokens_hbm, wq_hbm, wk_hbm, wv_hbm, out_hbm,
+    tok, weights, place, work, inbox, key_buf, value_buf, cos_buf, sin_buf, first_buf, staged,
+    tok_sem, w_sem, out_sem, send_sem, recv_sem,
+):
+    bits = shards.bit_length() - 1
+    chunks = heads_here // 2 + 1
+    tokens_total = tok.shape[0]
+    documents = len_ref.shape[0]
+    head = HEAD_SIZE
+    lag = 2
+    me = lax.axis_index("ctx")
+    column = lax.axis_index("tp")
+    orders = [list(range(bits)), list(reversed(range(bits)))]
+    inbox_at = [sum(shards >> (q + 1) for q in range(p)) * capacity for p in range(bits)]
+
+    def peer(bit):
+        step = 1 << bit
+        return me + step - 2 * step * ((me // step) % 2)
+
+    def flipped(mask):
+        ident = 0
+        for bit in range(bits):
+            own = (me // (1 << bit)) % 2
+            ident = ident + ((1 - own) if (mask >> bit) & 1 else own) * (1 << bit)
+        return ident
+
+    def mask_at(order, spot):
+        mask = 0
+        for p, bit in enumerate(order):
+            if (spot >> (bits - 1 - p)) & 1:
+                mask |= 1 << bit
+        return mask
+
+    def load_key_value():
+        return [
+            pltpu.make_async_copy(wk_hbm, weights.at[0, :, pl.ds(0, head)], w_sem.at[0]),
+            pltpu.make_async_copy(wv_hbm, weights.at[0, :, pl.ds(head, head)], w_sem.at[chunks]),
+        ]
+
+    def load_query(c):
+        at = pl.multiple_of((c - 1) * (2 * head), 2 * head)
+        return pltpu.make_async_copy(
+            wq_hbm.at[:, pl.ds(at, 2 * head)], weights.at[c], w_sem.at[c]
+        )
+
+    def send(c, half, p):
+        rows = (shards >> (p + 1)) * capacity
+        return pltpu.make_async_remote_copy(
+            src_ref=work.at[c, half, pl.ds(rows, rows)],
+            dst_ref=inbox.at[c, half, pl.ds(inbox_at[p], rows)],
+            send_sem=send_sem.at[c, half, p],
+            recv_sem=recv_sem.at[c, half, p],
+            device_id=(peer(orders[half][p]), column),
+            device_id_type=pl.DeviceIdType.MESH,
+        )
+
+    def store_out(c):
+        at = pl.multiple_of((c - 1) * (2 * head), 2 * head)
+        return pltpu.make_async_copy(
+            staged.at[c], out_hbm.at[:, pl.ds(at, 2 * head)], out_sem.at[c]
+        )
+
+    tok_copy = pltpu.make_async_copy(tokens_hbm, tok, tok_sem)
+    tok_copy.start()
+    for copy in load_key_value():
+        copy.start()
+    load_query(1).start()
+
+    barrier = pltpu.get_barrier_semaphore()
+    for bit in range(bits):
+        pl.semaphore_signal(
+            barrier, inc=1, device_id=(peer(bit), column), device_id_type=pl.DeviceIdType.MESH
+        )
+
+    token_ids = lax.broadcasted_iota(jnp.int32, (1, tokens_total), 1)
+    slot_ids = lax.broadcasted_iota(jnp.int32, (capacity, head), 0)
+
+    def place_document(d, carry):
+        start, target, first = carry
+        length = len_ref[d]
+        anchor = shard_ref[d] * capacity + slot_ref[d]
+        inside = (token_ids >= start) & (token_ids < start + length)
+        target = jnp.where(inside, anchor + token_ids - start, target)
+        slot = slot_ref[d]
+        here = jnp.where(shard_ref[d] == me, length, 0)
+        first = jnp.where((slot_ids >= slot) & (slot_ids < slot + here), slot, first)
+        return start + length, target, first
+
+    _, target, first = lax.fori_loop(
+        0, documents, place_document, (jnp.int32(0), jnp.zeros_like(token_ids), slot_ids)
+    )
+    first_buf[...] = first
+    local = lax.broadcasted_iota(jnp.int32, (capacity, tokens_total), 0)
+    for mask in range(shards):
+        hit = local + flipped(mask) * capacity == target
+        place[pl.ds(mask * capacity, capacity), :] = jnp.where(hit, 1.0, 0.0).astype(jnp.bfloat16)
+
+    pl.semaphore_wait(barrier, bits)
+    tok_copy.wait()
+
+    def produce(c):
+        term = jnp.dot(tok[...], weights[c], preferred_element_type=jnp.float32)
+        term = term.astype(jnp.bfloat16)
+        placed = jnp.dot(place[...], term, preferred_element_type=jnp.float32)
+        placed = placed.astype(jnp.bfloat16)
+        for half in range(2):
+            for spot in reversed(range(shards)):
+                mask = mask_at(orders[half], spot)
+                work[c, half, pl.ds(spot * capacity, capacity), :] = placed[
+                    mask * capacity : (mask + 1) * capacity, half * head : (half + 1) * head
+                ]
+        for half in range(2):
+            send(c, half, 0).start()
+
+    def gathered(c, half, spot, phases):
+        value = work[c, half, pl.ds(spot * capacity, capacity), :].astype(jnp.float32)
+        for p in range(phases):
+            value = value + inbox[
+                c, half, pl.ds(inbox_at[p] + spot * capacity, capacity), :
+            ].astype(jnp.float32)
+        return value
+
+    def relay(c, p):
+        for half in range(2):
+            send(c, half, p - 1).wait_recv()
+            for spot in range(shards >> (p + 1), shards >> p):
+                work[c, half, pl.ds(spot * capacity, capacity), :] = gathered(
+                    c, half, spot, p
+                ).astype(jnp.bfloat16)
+            send(c, half, p).start()
+
+    def rotate(value):
+        return value * cos_buf[...] + pltpu.roll(value, head // 2, 1) * sin_buf[...]
+
+    def take_key_value():
+        for half in range(2):
+            send(0, half, bits - 1).wait_recv()
+        angle = (slot_ids - first_buf[...]).astype(jnp.float32) * freq_ref[...]
+        lane = lax.broadcasted_iota(jnp.int32, (capacity, head), 1)
+        cos_buf[...] = jnp.cos(angle)
+        sine = jnp.sin(angle)
+        sin_buf[...] = jnp.where(lane < head // 2, -sine, sine)
+        key_raw = gathered(0, 0, 0, bits).astype(jnp.bfloat16).astype(jnp.float32)
+        key_buf[...] = rotate(key_raw).astype(jnp.bfloat16)
+        value_buf[...] = gathered(0, 1, 0, bits).astype(jnp.bfloat16)
+
+    def attend_heads(c):
+        for half in range(2):
+            send(c, half, bits - 1).wait_recv()
+        query = jnp.concatenate(
+            [rotate(gathered(c, half, 0, bits)).astype(jnp.bfloat16) for half in range(2)], axis=0
+        )
+        scores = lax.dot_general(
+            query, key_buf[...], (((1,), (1,)), ((), ())), preferred_element_type=jnp.float32
+        )
+        row = lax.broadcasted_iota(jnp.int32, (capacity, capacity), 0)
+        col = lax.broadcasted_iota(jnp.int32, (capacity, capacity), 1)
+        allowed = (col <= row) & (col >= first_buf[:, :1])
+        allowed = jnp.concatenate([allowed, allowed], axis=0)
+        scores = jnp.where(allowed, scores * (head**-0.5), -jnp.inf)
+        peak = jnp.max(scores, axis=-1, keepdims=True)
+        expo = jnp.exp(scores - peak)
+        total = jnp.sum(expo, axis=-1, keepdims=True)
+        mixed = jnp.dot(
+            expo.astype(jnp.bfloat16), value_buf[...], preferred_element_type=jnp.float32
+        )
+        result = (mixed / total).astype(jnp.bfloat16)
+        for half in range(2):
+            staged[c, :, half * head : (half + 1) * head] = result[
+                half * capacity : (half + 1) * capacity
+            ]
+        store_out(c).start()
+
+    def step(c, _):
+        @pl.when(c == 0)
+        def _():
+            for copy in load_key_value():
+                copy.wait()
+
+        @pl.when((c > 0) & (c < chunks))
+        def _():
+            load_query(c).wait()
+
+        @pl.when(c + 2 < chunks)
+        def _():
+            load_query(c + 2).start()
+
+        @pl.when(c < chunks)
+        def _():
+            produce(c)
+
+        for p in range(1, bits):
+            @pl.when((c >= lag * p) & (c < chunks + lag * p))
+            def _():
+                relay(c - lag * p, p)
+
+        @pl.when(c == lag * bits)
+        def _():
+            take_key_value()
+
+        @pl.when(c > lag * bits)
+        def _():
+            attend_heads(c - lag * bits)
+
+        return 0
+
+    lax.fori_loop(0, chunks + lag * bits, step, 0)
+
+    def finish(c, _):
+        for half in range(2):
+            for p in range(bits):
+                send(c, half, p).wait_send()
+
+        @pl.when(c > 0)
+        def _():
+            store_out(c).wait()
+
+        return 0
+
+    lax.fori_loop(0, chunks, finish, 0)
+
+
+def fused(tokens, wq, wk, wv, doc_len, doc_shard, doc_slot):
+    shards = lax.axis_size("ctx")
+    bits = shards.bit_length() - 1
+    total_tokens, depth = tokens.shape
+    per_shard = total_tokens // shards
+    capacity = per_shard + per_shard // 2
+    q_cols = wq.shape[1]
+    heads_here = q_cols // HEAD_SIZE
+    chunks = heads_here // 2 + 1
+    half = HEAD_SIZE // 2
+    freq = np.power(np.float32(rope_base), -np.arange(half, dtype=np.float32) * np.float32(2.0 / HEAD_SIZE))
+    freq = jnp.asarray(np.tile(freq, 2)[None, :], jnp.float32)
+    smem = pl.BlockSpec(memory_space=pltpu.SMEM)
+    hbm = pl.BlockSpec(memory_space=pl.ANY)
+    bf16 = jnp.bfloat16
+    return pl.pallas_call(
+        functools.partial(fused_kernel, shards, capacity, heads_here),
+        out_shape=jax.ShapeDtypeStruct((capacity, q_cols), bf16),
+        in_specs=[smem, smem, smem, pl.BlockSpec(memory_space=pltpu.VMEM), hbm, hbm, hbm, hbm],
+        out_specs=hbm,
+        scratch_shapes=[
+            pltpu.VMEM((total_tokens, depth), bf16),
+            pltpu.VMEM((chunks, depth, 2 * HEAD_SIZE), bf16),
+            pltpu.VMEM((shards * capacity, total_tokens), bf16),
+            pltpu.VMEM((chunks, 2, shards * capacity, HEAD_SIZE), bf16),
+            pltpu.VMEM((chunks, 2, (shards - 1) * capacity, HEAD_SIZE), bf16),
+            pltpu.VMEM((capacity, HEAD_SIZE), bf16),
+            pltpu.VMEM((capacity, HEAD_SIZE), bf16),
+            pltpu.VMEM((capacity, HEAD_SIZE), jnp.float32),
+            pltpu.VMEM((capacity, HEAD_SIZE), jnp.float32),
+            pltpu.VMEM((capacity, HEAD_SIZE), jnp.int32),
+            pltpu.VMEM((chunks, capacity, 2 * HEAD_SIZE), bf16),
+            pltpu.SemaphoreType.DMA,
+            pltpu.SemaphoreType.DMA((chunks + 1,)),
+            pltpu.SemaphoreType.DMA((chunks,)),
+            pltpu.SemaphoreType.DMA((chunks, 2, bits)),
+            pltpu.SemaphoreType.DMA((chunks, 2, bits)),
+        ],
+        compiler_params=pltpu.CompilerParams(
+            collective_id=0, has_side_effects=True, vmem_limit_bytes=56 * 2**20
+        ),
+        cost_estimate=pl.CostEstimate(
+            flops=2 * total_tokens * depth * (q_cols + 2 * HEAD_SIZE),
+            bytes_accessed=2 * depth * (total_tokens + q_cols + 2 * HEAD_SIZE),
+            transcendentals=0,
+        ),
+    )(doc_len, doc_shard, doc_slot, freq, tokens, wq, wk, wv)
+
+
+def body(tokens, wq, wk, wv, doc_len, doc_shard, doc_slot):
+    shards = lax.axis_size("ctx")
+    if wk.shape[1] == HEAD_SIZE and shards & (shards - 1) == 0:
+        return fused(tokens, wq, wk, wv, doc_len, doc_shard, doc_slot)
+    return plain(tokens, wq, wk, wv, doc_len, doc_shard, doc_slot)
+
+
 def solution(mesh):
     return jax.shard_map(
         body,

time: 121 us -> 42.7 us (0.35)
  waiting for transfers between devices: 46.7 us -> 0 us
  Pallas kernels: 0 us -> 40.5 us
  local copies, waits for them, and re-layouts: 28.5 us -> 2.09 us
  matrix products: 26 us -> 0 us
  between operations: 13.6 us -> 0.01 us
  other arithmetic: 5.74 us -> 0 us
    reduce_scatter x1 -> x0, waiting for transfers between devices: 46.7 us -> none  [body(): lax.psum_scatter(jnp.where(filled[:, None] == 1, partial_rows, jnp.float3...]
    pallas_call x0 -> x1, Pallas kernels: none -> 40.5 us  [fused(): pl.pallas_call(functools.partial(fused_kernel, shards, capacity, heads_he...]
    dot_general x3 -> x0, matrix products: 26 us -> none  [the longest x1 23.6 us: body(): partial_rows = jnp.dot(picked, joined, preferred_element_type=jnp.float32)]
    gather x1 -> x0, local copies, waits for them, and re-layouts: 14.8 us -> none  [body(): picked = jnp.take(tokens, source, axis=0)]
    scatter x4 -> x0, local copies, waits for them, and re-layouts: 10.2 us -> none  [the longest x1 2.67 us: slot_layout(): jnp.zeros((slot_total,), jnp.int32).at[target].set(position)]
    unnamed x1 -> x0, other arithmetic: 1.29 us -> none
  transfers between devices with their start and end apart: 1 -> 0, of which waited for: 1 -> 0; matrix products, arithmetic and copies ran while one was open for 3% -> 0% of each run, Pallas kernels for 0% -> 0%
where the time goes in v1:
time: 42.7 us; the launch traced here: 42.5 us
  Pallas kernels  40.5 us (95%)
  local copies, waits for them, and re-layouts  2.09 us (5%)
    pallas_call x1, Pallas kernels, fused(): pl.pallas_call(functools.partial(fused_kernel, shards, capacity, heads_he...  40.5 us
    unnamed x1, local copies, waits for them, and re-layouts  2.09 us

profile of v1, /device:TPU:0, one launch (start us, length us, event | category | flops | bytes accessed | tf_op | source)
XLA Modules:
  0.0 42.5 jit_solution(822684171254862294)
XLA Ops:
  0.0 40.5 %shard_map.82 = bf16[192,2048]{1,0:T(8,128)(2,1)} custom-call(s32[16]{0:T(128)} %len_ref.1, s32[16]{0:T(128)} %shard_ref.1, s32[16]{0:T(128)} %slot_ref.1, f32[1,128]{1,0:T(1,128)} %constant.2.clone.freq_ref, bf16[512,4096]{1,0:T(8,128)(2,1)} %tokens_hbm.1, bf16[4096,2048]{1,0:T(8,128)(2,1)} %wq_hbm.1, bf16[4096,128]{1,0:T(8,128)(2,1)} %wk_hbm.1, ...), custom_call_target="tpu_custom_call" | custom-call | flops 9663676416 | bytes 23068672 | tf_op jit(solution)/shard_map/pallas_call | solution.py:365
  40.5 2.1 %copy.10 = bf16[192,2048]{1,0:T(8,128)(2,1)} copy(bf16[192,2048]{1,0:T(8,128)(2,1)} %shard_map.82) | data formatting | bytes 1572864

commit v2 on v1

--- a/solution.py
+++ b/solution.py
@@ -125,13 +125,16 @@
 
 def fused_kernel(
     shards, capacity, heads_here,
-    len_ref, shard_ref, slot_ref, freq_ref, tokens_hbm, wq_hbm, wk_hbm, wv_hbm, out_hbm,
-    tok, weights, place, work, inbox, key_buf, value_buf, cos_buf, sin_buf, first_buf, staged,
-    tok_sem, w_sem, out_sem, send_sem, recv_sem,
+    len_hbm, shard_hbm, slot_hbm, freq_hbm, tokens_hbm, wq_hbm, wk_hbm, wv_hbm, out_ref,
+    len_ref, shard_ref, slot_ref, freq_ref, tok, weights, place, work, inbox, total_buf, term_buf,
+    key_buf, value_buf, cos_buf, sin_buf, first_buf,
+    table_sem, piece_sem, w_sem, send_sem, recv_sem,
 ):
     bits = shards.bit_length() - 1
     chunks = heads_here // 2 + 1
-    tokens_total = tok.shape[0]
+    tokens_total, depth = tok.shape
+    pieces = piece_sem.shape[0]
+    piece = depth // pieces
     documents = len_ref.shape[0]
     head = HEAD_SIZE
     lag = 2
@@ -158,10 +161,23 @@
                 mask |= 1 << bit
         return mask
 
-    def load_key_value():
+    tables = [
+        pltpu.make_async_copy(source, target, table_sem.at[i])
+        for i, (source, target) in enumerate(
+            [(len_hbm, len_ref), (shard_hbm, shard_ref), (slot_hbm, slot_ref), (freq_hbm, freq_ref)]
+        )
+    ]
+
+    def load_piece(k):
+        part = pl.ds(pl.multiple_of(k * piece, piece), piece)
         return [
-            pltpu.make_async_copy(wk_hbm, weights.at[0, :, pl.ds(0, head)], w_sem.at[0]),
-            pltpu.make_async_copy(wv_hbm, weights.at[0, :, pl.ds(head, head)], w_sem.at[chunks]),
+            pltpu.make_async_copy(tokens_hbm.at[:, part], tok.at[:, part], piece_sem.at[k, 0]),
+            pltpu.make_async_copy(
+                wk_hbm.at[part], weights.at[0, part, pl.ds(0, head)], piece_sem.at[k, 1]
+            ),
+            pltpu.make_async_copy(
+                wv_hbm.at[part], weights.at[0, part, pl.ds(head, head)], piece_sem.at[k, 2]
+            ),
         ]
 
     def load_query(c):
@@ -181,17 +197,11 @@
             device_id_type=pl.DeviceIdType.MESH,
         )
 
-    def store_out(c):
-        at = pl.multiple_of((c - 1) * (2 * head), 2 * head)
-        return pltpu.make_async_copy(
-            staged.at[c], out_hbm.at[:, pl.ds(at, 2 * head)], out_sem.at[c]
-        )
-
-    tok_copy = pltpu.make_async_copy(tokens_hbm, tok, tok_sem)
-    tok_copy.start()
-    for copy in load_key_value():
+    for copy in tables:
         copy.start()
-    load_query(1).start()
+    for k in range(pieces):
+        for copy in load_piece(k):
+            copy.start()
 
     barrier = pltpu.get_barrier_semaphore()
     for bit in range(bits):
@@ -201,6 +211,9 @@
 
     token_ids = lax.broadcasted_iota(jnp.int32, (1, tokens_total), 1)
     slot_ids = lax.broadcasted_iota(jnp.int32, (capacity, head), 0)
+
+    for copy in tables:
+        copy.wait()
 
     def place_document(d, carry):
         start, target, first = carry
@@ -222,13 +235,32 @@
         hit = local + flipped(mask) * capacity == target
         place[pl.ds(mask * capacity, capacity), :] = jnp.where(hit, 1.0, 0.0).astype(jnp.bfloat16)
 
-    pl.semaphore_wait(barrier, bits)
-    tok_copy.wait()
+    def first_product():
+        total_buf[...] = jnp.zeros_like(total_buf)
+
+        def add_piece(k, _):
+            for copy in load_piece(k):
+                copy.wait()
+            part = pl.ds(pl.multiple_of(k * piece, piece), piece)
+            total_buf[...] += jnp.dot(
+                tok[:, part], weights[0, part, :], preferred_element_type=jnp.float32
+            )
+            return 0
+
+        lax.fori_loop(0, pieces - 1, add_piece, 0)
+        load_query(1).start()
+        add_piece(pieces - 1, 0)
+        term_buf[...] = total_buf[...].astype(jnp.bfloat16)
+        pl.semaphore_wait(barrier, bits)
+
+    def product(c):
+        load_query(c).wait()
+        term_buf[...] = jnp.dot(
+            tok[...], weights[c], preferred_element_type=jnp.float32
+        ).astype(jnp.bfloat16)
 
     def produce(c):
-        term = jnp.dot(tok[...], weights[c], preferred_element_type=jnp.float32)
-        term = term.astype(jnp.bfloat16)
-        placed = jnp.dot(place[...], term, preferred_element_type=jnp.float32)
+        placed = jnp.dot(place[...], term_buf[...], preferred_element_type=jnp.float32)
         placed = placed.astype(jnp.bfloat16)
         for half in range(2):
             for spot in reversed(range(shards)):
@@ -284,29 +316,26 @@
         col = lax.broadcasted_iota(jnp.int32, (capacity, capacity), 1)
         allowed = (col <= row) & (col >= first_buf[:, :1])
         allowed = jnp.concatenate([allowed, allowed], axis=0)
-        scores = jnp.where(allowed, scores * (head**-0.5), -jnp.inf)
+        scores = jnp.where(allowed, scores, -jnp.inf)
         peak = jnp.max(scores, axis=-1, keepdims=True)
-        expo = jnp.exp(scores - peak)
+        expo = jnp.exp2((scores - peak) * (head**-0.5 * np.log2(np.e)))
         total = jnp.sum(expo, axis=-1, keepdims=True)
         mixed = jnp.dot(
             expo.astype(jnp.bfloat16), value_buf[...], preferred_element_type=jnp.float32
         )
         result = (mixed / total).astype(jnp.bfloat16)
         for half in range(2):
-            staged[c, :, half * head : (half + 1) * head] = result[
-                half * capacity : (half + 1) * capacity
-            ]
-        store_out(c).start()
+            at = pl.multiple_of((c - 1) * (2 * head) + half * head, head)
+            out_ref[:, pl.ds(at, head)] = result[half * capacity : (half + 1) * capacity]
 
     def step(c, _):
         @pl.when(c == 0)
         def _():
-            for copy in load_key_value():
-                copy.wait()
+            first_product()
 
         @pl.when((c > 0) & (c < chunks))
         def _():
-            load_query(c).wait()
+            product(c)
 
         @pl.when(c + 2 < chunks)
         def _():
@@ -337,11 +366,6 @@
         for half in range(2):
             for p in range(bits):
                 send(c, half, p).wait_send()
-
-        @pl.when(c > 0)
-        def _():
-            store_out(c).wait()
-
         return 0
 
     lax.fori_loop(0, chunks, finish, 0)
@@ -359,28 +383,33 @@
     half = HEAD_SIZE // 2
     freq = np.power(np.float32(rope_base), -np.arange(half, dtype=np.float32) * np.float32(2.0 / HEAD_SIZE))
     freq = jnp.asarray(np.tile(freq, 2)[None, :], jnp.float32)
-    smem = pl.BlockSpec(memory_space=pltpu.SMEM)
+    documents = doc_len.shape[0]
     hbm = pl.BlockSpec(memory_space=pl.ANY)
     bf16 = jnp.bfloat16
     return pl.pallas_call(
         functools.partial(fused_kernel, shards, capacity, heads_here),
-        out_shape=jax.ShapeDtypeStruct((capacity, q_cols), bf16),
-        in_specs=[smem, smem, smem, pl.BlockSpec(memory_space=pltpu.VMEM), hbm, hbm, hbm, hbm],
-        out_specs=hbm,
+        out_shape=pltpu.VMEM((capacity, q_cols), bf16),
+        in_specs=[hbm] * 8,
+        out_specs=pl.BlockSpec(memory_space=pltpu.VMEM),
         scratch_shapes=[
+            pltpu.SMEM((documents,), jnp.int32),
+            pltpu.SMEM((documents,), jnp.int32),
+            pltpu.SMEM((documents,), jnp.int32),
+            pltpu.VMEM((1, HEAD_SIZE), jnp.float32),
             pltpu.VMEM((total_tokens, depth), bf16),
             pltpu.VMEM((chunks, depth, 2 * HEAD_SIZE), bf16),
             pltpu.VMEM((shards * capacity, total_tokens), bf16),
             pltpu.VMEM((chunks, 2, shards * capacity, HEAD_SIZE), bf16),
             pltpu.VMEM((chunks, 2, (shards - 1) * capacity, HEAD_SIZE), bf16),
+            pltpu.VMEM((total_tokens, 2 * HEAD_SIZE), jnp.float32),
+            pltpu.VMEM((total_tokens, 2 * HEAD_SIZE), bf16),
             pltpu.VMEM((capacity, HEAD_SIZE), bf16),
             pltpu.VMEM((capacity, HEAD_SIZE), bf16),
             pltpu.VMEM((capacity, HEAD_SIZE), jnp.float32),
             pltpu.VMEM((capacity, HEAD_SIZE), jnp.float32),
             pltpu.VMEM((capacity, HEAD_SIZE), jnp.int32),
-            pltpu.VMEM((chunks, capacity, 2 * HEAD_SIZE), bf16),
-            pltpu.SemaphoreType.DMA,
-            pltpu.SemaphoreType.DMA((chunks + 1,)),
+            pltpu.SemaphoreType.DMA((4,)),
+            pltpu.SemaphoreType.DMA((4, 3)),
             pltpu.SemaphoreType.DMA((chunks,)),
             pltpu.SemaphoreType.DMA((chunks, 2, bits)),
             pltpu.SemaphoreType.DMA((chunks, 2, bits)),

time: 42.7 us -> 41 us (0.960)
  local copies, waits for them, and re-layouts: 2.09 us -> 0.88 us
  Pallas kernels: 40.5 us -> 40 us
    unnamed x1, local copies, waits for them, and re-layouts: 2.09 us -> 0.88 us
    pallas_call x1, Pallas kernels: 40.5 us -> 40 us  [fused(): pl.pallas_call(functools.partial(fused_kernel, shards, capacity, heads_he...]
where the time goes in v2:
time: 41 us; the launch traced here: 40.9 us
  Pallas kernels  40 us (98%)
  local copies, waits for them, and re-layouts  0.88 us (2%)
    pallas_call x1, Pallas kernels, fused(): pl.pallas_call(functools.partial(fused_kernel, shards, capacity, heads_he...  40 us
    unnamed x1, local copies, waits for them, and re-layouts  0.88 us

profile of v2, /device:TPU:0, one launch (start us, length us, event | category | flops | bytes accessed | tf_op | source)
XLA Modules:
  0.0 40.9 jit_solution(7065336256419781674)
XLA Ops:
  0.0 40.0 %shard_map.82 = bf16[192,2048]{1,0:T(8,128)(2,1)S(1)} custom-call(s32[16]{0:T(128)} %len_hbm.1, s32[16]{0:T(128)} %shard_hbm.1, s32[16]{0:T(128)} %slot_hbm.1, f32[1,128]{1,0:T(1,128)} %constant.2.clone.freq_hbm, bf16[512,4096]{1,0:T(8,128)(2,1)} %tokens_hbm.1, bf16[4096,2048]{1,0:T(8,128)(2,1)} %wq_hbm.1, bf16[4096,128]{1,0:T(8,128)(2,1)} %wk_hbm.1, ...), custom_call_target="tpu_custom_call" | custom-call | flops 9663676416 | bytes 23068672 | tf_op jit(solution)/shard_map/pallas_call | solution.py:389
  40.0 0.9 %copy.10 = bf16[192,2048]{1,0:T(8,128)(2,1)} copy(bf16[192,2048]{1,0:T(8,128)(2,1)S(1)} %shard_map.82) | data formatting | bytes 1572864

commit v3 on v2

--- a/solution.py
+++ b/solution.py
@@ -127,7 +127,7 @@
     shards, capacity, heads_here,
     len_hbm, shard_hbm, slot_hbm, freq_hbm, tokens_hbm, wq_hbm, wk_hbm, wv_hbm, out_ref,
     len_ref, shard_ref, slot_ref, freq_ref, tok, weights, place, work, inbox, total_buf, term_buf,
-    key_buf, value_buf, cos_buf, sin_buf, first_buf,
+    key_buf, value_buf, cos_buf, sin_buf, first_buf, mask_buf,
     table_sem, piece_sem, w_sem, send_sem, recv_sem,
 ):
     bits = shards.bit_length() - 1
@@ -292,8 +292,7 @@
         return value * cos_buf[...] + pltpu.roll(value, head // 2, 1) * sin_buf[...]
 
     def take_key_value():
-        for half in range(2):
-            send(0, half, bits - 1).wait_recv()
+        wait_last(0)
         angle = (slot_ids - first_buf[...]).astype(jnp.float32) * freq_ref[...]
         lane = lax.broadcasted_iota(jnp.int32, (capacity, head), 1)
         cos_buf[...] = jnp.cos(angle)
@@ -301,32 +300,39 @@
         sin_buf[...] = jnp.where(lane < head // 2, -sine, sine)
         key_raw = gathered(0, 0, 0, bits).astype(jnp.bfloat16).astype(jnp.float32)
         key_buf[...] = rotate(key_raw).astype(jnp.bfloat16)
-        value_buf[...] = gathered(0, 1, 0, bits).astype(jnp.bfloat16)
-
-    def attend_heads(c):
-        for half in range(2):
-            send(c, half, bits - 1).wait_recv()
-        query = jnp.concatenate(
-            [rotate(gathered(c, half, 0, bits)).astype(jnp.bfloat16) for half in range(2)], axis=0
-        )
-        scores = lax.dot_general(
-            query, key_buf[...], (((1,), (1,)), ((), ())), preferred_element_type=jnp.float32
-        )
+        value_buf[:, :head] = gathered(0, 1, 0, bits).astype(jnp.bfloat16)
+        value_buf[:, head:] = jnp.ones((capacity, head), jnp.bfloat16)
         row = lax.broadcasted_iota(jnp.int32, (capacity, capacity), 0)
         col = lax.broadcasted_iota(jnp.int32, (capacity, capacity), 1)
         allowed = (col <= row) & (col >= first_buf[:, :1])
-        allowed = jnp.concatenate([allowed, allowed], axis=0)
-        scores = jnp.where(allowed, scores, -jnp.inf)
-        peak = jnp.max(scores, axis=-1, keepdims=True)
-        expo = jnp.exp2((scores - peak) * (head**-0.5 * np.log2(np.e)))
-        total = jnp.sum(expo, axis=-1, keepdims=True)
-        mixed = jnp.dot(
-            expo.astype(jnp.bfloat16), value_buf[...], preferred_element_type=jnp.float32
-        )
-        result = (mixed / total).astype(jnp.bfloat16)
+        mask_buf[...] = jnp.where(allowed, 0.0, -jnp.inf)
+
+    def attend_heads(c):
+        query = [rotate(gathered(c, half, 0, bits)).astype(jnp.bfloat16) for half in range(2)]
+        for low in range(0, capacity, head):
+            high = min(low + head, capacity)
+            rows = high - low
+            scores = lax.dot_general(
+                jnp.concatenate([q[low:high] for q in query], axis=0),
+                key_buf[:high],
+                (((1,), (1,)), ((), ())),
+                preferred_element_type=jnp.float32,
+            )
+            mask = mask_buf[low:high, :high]
+            scores = scores + jnp.concatenate([mask, mask], axis=0)
+            peak = jnp.max(scores, axis=-1, keepdims=True)
+            expo = jnp.exp2((scores - peak) * (head**-0.5 * np.log2(np.e)))
+            mixed = jnp.dot(
+                expo.astype(jnp.bfloat16), value_buf[:high], preferred_element_type=jnp.float32
+            )
+            result = (mixed[:, :head] / mixed[:, head:]).astype(jnp.bfloat16)
+            for half in range(2):
+                at = pl.multiple_of((c - 1) * (2 * head) + half * head, head)
+                out_ref[low:high, pl.ds(at, head)] = result[half * rows : (half + 1) * rows]
+
+    def wait_last(c):
         for half in range(2):
-            at = pl.multiple_of((c - 1) * (2 * head) + half * head, head)
-            out_ref[:, pl.ds(at, head)] = result[half * capacity : (half + 1) * capacity]
+            send(c, half, bits - 1).wait_recv()
 
     def step(c, _):
         @pl.when(c == 0)
@@ -356,11 +362,31 @@
 
         @pl.when(c > lag * bits)
         def _():
+            wait_last(c - lag * bits)
             attend_heads(c - lag * bits)
 
         return 0
 
-    lax.fori_loop(0, chunks + lag * bits, step, 0)
+    def steady_step(c, _):
+        for p in reversed(range(1, bits)):
+            relay(c - lag * p, p)
+        wait_last(c - lag * bits)
+        load_query(c).wait()
+        term = jnp.dot(tok[...], weights[c], preferred_element_type=jnp.float32)
+        attend_heads(c - lag * bits)
+        term_buf[...] = term.astype(jnp.bfloat16)
+        produce(c)
+
+        @pl.when(c + 2 < chunks)
+        def _():
+            load_query(c + 2).start()
+
+        return 0
+
+    begin = min(lag * bits + 1, chunks)
+    lax.fori_loop(0, begin, step, 0)
+    lax.fori_loop(begin, chunks, steady_step, 0)
+    lax.fori_loop(chunks, chunks + lag * bits, step, 0)
 
     def finish(c, _):
         for half in range(2):
@@ -404,10 +430,11 @@
             pltpu.VMEM((total_tokens, 2 * HEAD_SIZE), jnp.float32),
             pltpu.VMEM((total_tokens, 2 * HEAD_SIZE), bf16),
             pltpu.VMEM((capacity, HEAD_SIZE), bf16),
-            pltpu.VMEM((capacity, HEAD_SIZE), bf16),
+            pltpu.VMEM((capacity, 2 * HEAD_SIZE), bf16),
             pltpu.VMEM((capacity, HEAD_SIZE), jnp.float32),
             pltpu.VMEM((capacity, HEAD_SIZE), jnp.float32),
             pltpu.VMEM((capacity, HEAD_SIZE), jnp.int32),
+            pltpu.VMEM((capacity, capacity), jnp.float32),
             pltpu.SemaphoreType.DMA((4,)),
             pltpu.SemaphoreType.DMA((4, 3)),
             pltpu.SemaphoreType.DMA((chunks,)),

time: 41 us -> 42.1 us (1.027)
  Pallas kernels: 40 us -> 41 us
    pallas_call x1, Pallas kernels: 40 us -> 41 us  [fused(): pl.pallas_call(functools.partial(fused_kernel, shards, capacity, heads_he...]
where the time goes in v3:
time: 42.1 us; the launch traced here: 41.9 us
  Pallas kernels  41 us (97%)
  local copies, waits for them, and re-layouts  0.88 us (2%)
    pallas_call x1, Pallas kernels, fused(): pl.pallas_call(functools.partial(fused_kernel, shards, capacity, heads_he...  41 us
    unnamed x1, local copies, waits for them, and re-layouts  0.88 us

profile of v3, /device:TPU:0, one launch (start us, length us, event | category | flops | bytes accessed | tf_op | source)
XLA Modules:
  0.0 41.9 jit_solution(9765952084808075159)
XLA Ops:
  0.0 41.0 %shard_map.82 = bf16[192,2048]{1,0:T(8,128)(2,1)S(1)} custom-call(s32[16]{0:T(128)} %len_hbm.1, s32[16]{0:T(128)} %shard_hbm.1, s32[16]{0:T(128)} %slot_hbm.1, f32[1,128]{1,0:T(1,128)} %constant.2.clone.freq_hbm, bf16[512,4096]{1,0:T(8,128)(2,1)} %tokens_hbm.1, bf16[4096,2048]{1,0:T(8,128)(2,1)} %wq_hbm.1, bf16[4096,128]{1,0:T(8,128)(2,1)} %wk_hbm.1, ...), custom_call_target="tpu_custom_call" | custom-call | flops 9663676416 | bytes 23068672 | tf_op jit(solution)/shard_map/pallas_call | solution.py:415
  41.0 0.9 %copy.10 = bf16[192,2048]{1,0:T(8,128)(2,1)} copy(bf16[192,2048]{1,0:T(8,128)(2,1)S(1)} %shard_map.82) | data formatting | bytes 1572864

commit v4 on v3

--- a/solution.py
+++ b/solution.py
@@ -137,7 +137,8 @@
     piece = depth // pieces
     documents = len_ref.shape[0]
     head = HEAD_SIZE
-    lag = 2
+    lags = [2 * p + 1 for p in range(bits + 1)]
+    last_lag = lags[bits]
     me = lax.axis_index("ctx")
     column = lax.axis_index("tp")
     orders = [list(range(bits)), list(reversed(range(bits)))]
@@ -169,7 +170,7 @@
     ]
 
     def load_piece(k):
-        part = pl.ds(pl.multiple_of(k * piece, piece), piece)
+        part = pl.ds(k * piece, piece)
         return [
             pltpu.make_async_copy(tokens_hbm.at[:, part], tok.at[:, part], piece_sem.at[k, 0]),
             pltpu.make_async_copy(
@@ -216,41 +217,46 @@
         copy.wait()
 
     def place_document(d, carry):
-        start, target, first = carry
+        start, target = carry
         length = len_ref[d]
         anchor = shard_ref[d] * capacity + slot_ref[d]
         inside = (token_ids >= start) & (token_ids < start + length)
         target = jnp.where(inside, anchor + token_ids - start, target)
+        return start + length, target
+
+    _, target = lax.fori_loop(
+        0, documents, place_document, (jnp.int32(0), jnp.zeros_like(token_ids))
+    )
+
+    def build_place():
+        local = lax.broadcasted_iota(jnp.int32, (capacity, tokens_total), 0)
+        for mask in range(shards):
+            hit = local == target - flipped(mask) * capacity
+            place[pl.ds(mask * capacity, capacity), :] = jnp.where(hit, 1.0, 0.0).astype(
+                jnp.bfloat16
+            )
+
+    def first_slot(d, first):
         slot = slot_ref[d]
-        here = jnp.where(shard_ref[d] == me, length, 0)
-        first = jnp.where((slot_ids >= slot) & (slot_ids < slot + here), slot, first)
-        return start + length, target, first
-
-    _, target, first = lax.fori_loop(
-        0, documents, place_document, (jnp.int32(0), jnp.zeros_like(token_ids), slot_ids)
-    )
-    first_buf[...] = first
-    local = lax.broadcasted_iota(jnp.int32, (capacity, tokens_total), 0)
-    for mask in range(shards):
-        hit = local + flipped(mask) * capacity == target
-        place[pl.ds(mask * capacity, capacity), :] = jnp.where(hit, 1.0, 0.0).astype(jnp.bfloat16)
+        here = jnp.where(shard_ref[d] == me, len_ref[d], 0)
+        return jnp.where((slot_ids >= slot) & (slot_ids < slot + here), slot, first)
 
     def first_product():
-        total_buf[...] = jnp.zeros_like(total_buf)
-
-        def add_piece(k, _):
+        for k in range(pieces):
+            if k == pieces - 1:
+                load_query(1).start()
+                build_place()
             for copy in load_piece(k):
                 copy.wait()
-            part = pl.ds(pl.multiple_of(k * piece, piece), piece)
-            total_buf[...] += jnp.dot(
+            part = pl.ds(k * piece, piece)
+            term = jnp.dot(
                 tok[:, part], weights[0, part, :], preferred_element_type=jnp.float32
             )
-            return 0
-
-        lax.fori_loop(0, pieces - 1, add_piece, 0)
-        load_query(1).start()
-        add_piece(pieces - 1, 0)
-        term_buf[...] = total_buf[...].astype(jnp.bfloat16)
+            if k > 0:
+                term = total_buf[...] + term
+            if k < pieces - 1:
+                total_buf[...] = term
+        term_buf[...] = term.astype(jnp.bfloat16)
         pl.semaphore_wait(barrier, bits)
 
     def product(c):
@@ -293,7 +299,9 @@
 
     def take_key_value():
         wait_last(0)
-        angle = (slot_ids - first_buf[...]).astype(jnp.float32) * freq_ref[...]
+        first = lax.fori_loop(0, documents, first_slot, slot_ids)
+        first_buf[...] = first
+        angle = (slot_ids - first).astype(jnp.float32) * freq_ref[...]
         lane = lax.broadcasted_iota(jnp.int32, (capacity, head), 1)
         cos_buf[...] = jnp.cos(angle)
         sine = jnp.sin(angle)
@@ -352,41 +360,22 @@
             produce(c)
 
         for p in range(1, bits):
-            @pl.when((c >= lag * p) & (c < chunks + lag * p))
+            @pl.when((c >= lags[p]) & (c < chunks + lags[p]))
             def _():
-                relay(c - lag * p, p)
-
-        @pl.when(c == lag * bits)
+                relay(c - lags[p], p)
+
+        @pl.when(c == last_lag)
         def _():
             take_key_value()
 
-        @pl.when(c > lag * bits)
-        def _():
-            wait_last(c - lag * bits)
-            attend_heads(c - lag * bits)
+        @pl.when(c > last_lag)
+        def _():
+            wait_last(c - last_lag)
+            attend_heads(c - last_lag)
 
         return 0
 
-    def steady_step(c, _):
-        for p in reversed(range(1, bits)):
-            relay(c - lag * p, p)
-        wait_last(c - lag * bits)
-        load_query(c).wait()
-        term = jnp.dot(tok[...], weights[c], preferred_element_type=jnp.float32)
-        attend_heads(c - lag * bits)
-        term_buf[...] = term.astype(jnp.bfloat16)
-        produce(c)
-
-        @pl.when(c + 2 < chunks)
-        def _():
-            load_query(c + 2).start()
-
-        return 0
-
-    begin = min(lag * bits + 1, chunks)
-    lax.fori_loop(0, begin, step, 0)
-    lax.fori_loop(begin, chunks, steady_step, 0)
-    lax.fori_loop(chunks, chunks + lag * bits, step, 0)
+    lax.fori_loop(0, chunks + last_lag, step, 0)
 
     def finish(c, _):
         for half in range(2):

time: 42.1 us -> 42 us (level)
  no operation moved by 1% of the time
where the time goes in v4:
time: 42 us; the launch traced here: 41.8 us
  Pallas kernels  40.9 us (97%)
  local copies, waits for them, and re-layouts  0.88 us (2%)
    pallas_call x1, Pallas kernels, fused(): pl.pallas_call(functools.partial(fused_kernel, shards, capacity, heads_he...  40.9 us
    unnamed x1, local copies, waits for them, and re-layouts  0.88 us

profile of v4, /device:TPU:0, one launch (start us, length us, event | category | flops | bytes accessed | tf_op | source)
XLA Modules:
  0.0 41.8 jit_solution(12381254262029496054)
XLA Ops:
  0.0 40.9 %shard_map.82 = bf16[192,2048]{1,0:T(8,128)(2,1)S(1)} custom-call(s32[16]{0:T(128)} %len_hbm.1, s32[16]{0:T(128)} %shard_hbm.1, s32[16]{0:T(128)} %slot_hbm.1, f32[1,128]{1,0:T(1,128)} %constant.2.clone.freq_hbm, bf16[512,4096]{1,0:T(8,128)(2,1)} %tokens_hbm.1, bf16[4096,2048]{1,0:T(8,128)(2,1)} %wq_hbm.1, bf16[4096,128]{1,0:T(8,128)(2,1)} %wk_hbm.1, ...), custom_call_target="tpu_custom_call" | custom-call | flops 9663676416 | bytes 23068672 | tf_op jit(solution)/shard_map/pallas_call | solution.py:404
  40.9 0.9 %copy.10 = bf16[192,2048]{1,0:T(8,128)(2,1)} copy(bf16[192,2048]{1,0:T(8,128)(2,1)S(1)} %shard_map.82) | data formatting | bytes 1572864

commit v5 on v4

--- a/solution.py
+++ b/solution.py
@@ -132,12 +132,14 @@
 ):
     bits = shards.bit_length() - 1
     chunks = heads_here // 2 + 1
+    groups = heads_here // 4 + 1
+    wide = 4 * HEAD_SIZE
     tokens_total, depth = tok.shape
     pieces = piece_sem.shape[0]
     piece = depth // pieces
     documents = len_ref.shape[0]
     head = HEAD_SIZE
-    lags = [2 * p + 1 for p in range(bits + 1)]
+    lags = [2 * p - (p == bits) for p in range(bits + 1)]
     last_lag = lags[bits]
     me = lax.axis_index("ctx")
     column = lax.axis_index("tp")
@@ -181,11 +183,9 @@
             ),
         ]
 
-    def load_query(c):
-        at = pl.multiple_of((c - 1) * (2 * head), 2 * head)
-        return pltpu.make_async_copy(
-            wq_hbm.at[:, pl.ds(at, 2 * head)], weights.at[c], w_sem.at[c]
-        )
+    def load_query(g):
+        at = pl.multiple_of((g - 1) * wide, wide)
+        return pltpu.make_async_copy(wq_hbm.at[:, pl.ds(at, wide)], weights.at[g], w_sem.at[g])
 
     def send(c, half, p):
         rows = (shards >> (p + 1)) * capacity
@@ -250,23 +250,26 @@
                 copy.wait()
             part = pl.ds(k * piece, piece)
             term = jnp.dot(
-                tok[:, part], weights[0, part, :], preferred_element_type=jnp.float32
+                tok[:, part], weights[0, part, : 2 * head], preferred_element_type=jnp.float32
             )
             if k > 0:
                 term = total_buf[...] + term
             if k < pieces - 1:
                 total_buf[...] = term
-        term_buf[...] = term.astype(jnp.bfloat16)
+        term_buf[1] = term.astype(jnp.bfloat16)
         pl.semaphore_wait(barrier, bits)
 
-    def product(c):
-        load_query(c).wait()
-        term_buf[...] = jnp.dot(
-            tok[...], weights[c], preferred_element_type=jnp.float32
-        ).astype(jnp.bfloat16)
+    def product(g):
+        load_query(g).wait()
+        term = jnp.dot(tok[...], weights[g], preferred_element_type=jnp.float32)
+        term = term.astype(jnp.bfloat16)
+        term_buf[0] = term[:, : 2 * head]
+        term_buf[1] = term[:, 2 * head :]
 
     def produce(c):
-        placed = jnp.dot(place[...], term_buf[...], preferred_element_type=jnp.float32)
+        placed = jnp.dot(
+            place[...], term_buf[(c + 1) % 2], preferred_element_type=jnp.float32
+        )
         placed = placed.astype(jnp.bfloat16)
         for half in range(2):
             for spot in reversed(range(shards)):
@@ -308,8 +311,7 @@
         sin_buf[...] = jnp.where(lane < head // 2, -sine, sine)
         key_raw = gathered(0, 0, 0, bits).astype(jnp.bfloat16).astype(jnp.float32)
         key_buf[...] = rotate(key_raw).astype(jnp.bfloat16)
-        value_buf[:, :head] = gathered(0, 1, 0, bits).astype(jnp.bfloat16)
-        value_buf[:, head:] = jnp.ones((capacity, head), jnp.bfloat16)
+        value_buf[...] = gathered(0, 1, 0, bits).astype(jnp.bfloat16)
         row = lax.broadcasted_iota(jnp.int32, (capacity, capacity), 0)
         col = lax.broadcasted_iota(jnp.int32, (capacity, capacity), 1)
         allowed = (col <= row) & (col >= first_buf[:, :1])
@@ -317,26 +319,23 @@
 
     def attend_heads(c):
         query = [rotate(gathered(c, half, 0, bits)).astype(jnp.bfloat16) for half in range(2)]
-        for low in range(0, capacity, head):
-            high = min(low + head, capacity)
-            rows = high - low
-            scores = lax.dot_general(
-                jnp.concatenate([q[low:high] for q in query], axis=0),
-                key_buf[:high],
-                (((1,), (1,)), ((), ())),
-                preferred_element_type=jnp.float32,
-            )
-            mask = mask_buf[low:high, :high]
-            scores = scores + jnp.concatenate([mask, mask], axis=0)
-            peak = jnp.max(scores, axis=-1, keepdims=True)
-            expo = jnp.exp2((scores - peak) * (head**-0.5 * np.log2(np.e)))
-            mixed = jnp.dot(
-                expo.astype(jnp.bfloat16), value_buf[:high], preferred_element_type=jnp.float32
-            )
-            result = (mixed[:, :head] / mixed[:, head:]).astype(jnp.bfloat16)
-            for half in range(2):
-                at = pl.multiple_of((c - 1) * (2 * head) + half * head, head)
-                out_ref[low:high, pl.ds(at, head)] = result[half * rows : (half + 1) * rows]
+        scores = lax.dot_general(
+            jnp.concatenate(query, axis=0),
+            key_buf[...],
+            (((1,), (1,)), ((), ())),
+            preferred_element_type=jnp.float32,
+        )
+        scores = scores + jnp.concatenate([mask_buf[...], mask_buf[...]], axis=0)
+        peak = jnp.max(scores, axis=-1, keepdims=True)
+        expo = jnp.exp2((scores - peak) * (head**-0.5 * np.log2(np.e)))
+        total = jnp.sum(expo, axis=-1, keepdims=True)
+        mixed = jnp.dot(
+            expo.astype(jnp.bfloat16), value_buf[...], preferred_element_type=jnp.float32
+        )
+        result = (mixed / total).astype(jnp.bfloat16)
+        for half in range(2):
+            at = pl.multiple_of((c - 1) * (2 * head) + half * head, head)
+            out_ref[:, pl.ds(at, head)] = result[half * capacity : (half + 1) * capacity]
 
     def wait_last(c):
         for half in range(2):
@@ -347,13 +346,13 @@
         def _():
             first_product()
 
-        @pl.when((c > 0) & (c < chunks))
-        def _():
-            product(c)
-
-        @pl.when(c + 2 < chunks)
-        def _():
-            load_query(c + 2).start()
+        @pl.when((c % 2 == 1) & (c < chunks))
+        def _():
+            product((c + 1) // 2)
+
+        @pl.when((c % 2 == 1) & ((c + 1) // 2 + 1 < groups))
+        def _():
+            load_query((c + 1) // 2 + 1).start()
 
         @pl.when(c < chunks)
         def _():
@@ -395,6 +394,7 @@
     q_cols = wq.shape[1]
     heads_here = q_cols // HEAD_SIZE
     chunks = heads_here // 2 + 1
+    groups = heads_here // 4 + 1
     half = HEAD_SIZE // 2
     freq = np.power(np.float32(rope_base), -np.arange(half, dtype=np.float32) * np.float32(2.0 / HEAD_SIZE))
     freq = jnp.asarray(np.tile(freq, 2)[None, :], jnp.float32)
@@ -412,21 +412,21 @@
             pltpu.SMEM((documents,), jnp.int32),
             pltpu.VMEM((1, HEAD_SIZE), jnp.float32),
             pltpu.VMEM((total_tokens, depth), bf16),
-            pltpu.VMEM((chunks, depth, 2 * HEAD_SIZE), bf16),
+            pltpu.VMEM((groups, depth, 4 * HEAD_SIZE), bf16),
             pltpu.VMEM((shards * capacity, total_tokens), bf16),
             pltpu.VMEM((chunks, 2, shards * capacity, HEAD_SIZE), bf16),
             pltpu.VMEM((chunks, 2, (shards - 1) * capacity, HEAD_SIZE), bf16),
             pltpu.VMEM((total_tokens, 2 * HEAD_SIZE), jnp.float32),
-            pltpu.VMEM((total_tokens, 2 * HEAD_SIZE), bf16),
+            pltpu.VMEM((2, total_tokens, 2 * HEAD_SIZE), bf16),
             pltpu.VMEM((capacity, HEAD_SIZE), bf16),
-            pltpu.VMEM((capacity, 2 * HEAD_SIZE), bf16),
+            pltpu.VMEM((capacity, HEAD_SIZE), bf16),
             pltpu.VMEM((capacity, HEAD_SIZE), jnp.float32),
             pltpu.VMEM((capacity, HEAD_SIZE), jnp.float32),
             pltpu.VMEM((capacity, HEAD_SIZE), jnp.int32),
             pltpu.VMEM((capacity, capacity), jnp.float32),
             pltpu.SemaphoreType.DMA((4,)),
             pltpu.SemaphoreType.DMA((4, 3)),
-            pltpu.SemaphoreType.DMA((chunks,)),
+            pltpu.SemaphoreType.DMA((groups,)),
             pltpu.SemaphoreType.DMA((chunks, 2, bits)),
             pltpu.SemaphoreType.DMA((chunks, 2, bits)),
         ],
@@ -443,7 +443,8 @@
 
 def body(tokens, wq, wk, wv, doc_len, doc_shard, doc_slot):
     shards = lax.axis_size("ctx")
-    if wk.shape[1] == HEAD_SIZE and shards & (shards - 1) == 0:
+    whole_groups = wq.shape[1] % (4 * HEAD_SIZE) == 0
+    if wk.shape[1] == HEAD_SIZE and shards & (shards - 1) == 0 and whole_groups:
         return fused(tokens, wq, wk, wv, doc_len, doc_shard, doc_slot)
     return plain(tokens, wq, wk, wv, doc_len, doc_shard, doc_slot)
 

time: 42 us -> 47.1 us (1.12)
  Pallas kernels: 40.9 us -> 46.1 us
    pallas_call x1, Pallas kernels: 40.9 us -> 46.1 us  [fused(): pl.pallas_call(functools.partial(fused_kernel, shards, capacity, heads_he...]
where the time goes in v5:
time: 47.1 us; the launch traced here: 47 us
  Pallas kernels  46.1 us (98%)
  local copies, waits for them, and re-layouts  0.88 us (2%)
    pallas_call x1, Pallas kernels, fused(): pl.pallas_call(functools.partial(fused_kernel, shards, capacity, heads_he...  46.1 us

profile of v5, /device:TPU:0, one launch (start us, length us, event | category | flops | bytes accessed | tf_op | source)
XLA Modules:
  0.0 47.0 jit_solution(4542805541860100049)
XLA Ops:
  0.0 46.1 %shard_map.82 = bf16[192,2048]{1,0:T(8,128)(2,1)S(1)} custom-call(s32[16]{0:T(128)} %len_hbm.1, s32[16]{0:T(128)} %shard_hbm.1, s32[16]{0:T(128)} %slot_hbm.1, f32[1,128]{1,0:T(1,128)} %constant.2.clone.freq_hbm, bf16[512,4096]{1,0:T(8,128)(2,1)} %tokens_hbm.1, bf16[4096,2048]{1,0:T(8,128)(2,1)} %wq_hbm.1, bf16[4096,128]{1,0:T(8,128)(2,1)} %wk_hbm.1, ...), custom_call_target="tpu_custom_call" | custom-call | flops 9663676416 | bytes 23068672 | tf_op jit(solution)/shard_map/pallas_call | solution.py:404
  46.1 0.9 %copy.10 = bf16[192,2048]{1,0:T(8,128)(2,1)} copy(bf16[192,2048]{1,0:T(8,128)(2,1)S(1)} %shard_map.82) | data formatting | bytes 1572864

commit v6 on v4

--- a/solution.py
+++ b/solution.py
@@ -137,7 +137,7 @@
     piece = depth // pieces
     documents = len_ref.shape[0]
     head = HEAD_SIZE
-    lags = [2 * p + 1 for p in range(bits + 1)]
+    lags = [2 * p for p in range(bits + 1)]
     last_lag = lags[bits]
     me = lax.axis_index("ctx")
     column = lax.axis_index("tp")
@@ -308,8 +308,7 @@
         sin_buf[...] = jnp.where(lane < head // 2, -sine, sine)
         key_raw = gathered(0, 0, 0, bits).astype(jnp.bfloat16).astype(jnp.float32)
         key_buf[...] = rotate(key_raw).astype(jnp.bfloat16)
-        value_buf[:, :head] = gathered(0, 1, 0, bits).astype(jnp.bfloat16)
-        value_buf[:, head:] = jnp.ones((capacity, head), jnp.bfloat16)
+        value_buf[...] = gathered(0, 1, 0, bits).astype(jnp.bfloat16)
         row = lax.broadcasted_iota(jnp.int32, (capacity, capacity), 0)
         col = lax.broadcasted_iota(jnp.int32, (capacity, capacity), 1)
         allowed = (col <= row) & (col >= first_buf[:, :1])
@@ -317,26 +316,23 @@
 
     def attend_heads(c):
         query = [rotate(gathered(c, half, 0, bits)).astype(jnp.bfloat16) for half in range(2)]
-        for low in range(0, capacity, head):
-            high = min(low + head, capacity)
-            rows = high - low
-            scores = lax.dot_general(
-                jnp.concatenate([q[low:high] for q in query], axis=0),
-                key_buf[:high],
-                (((1,), (1,)), ((), ())),
-                preferred_element_type=jnp.float32,
-            )
-            mask = mask_buf[low:high, :high]
-            scores = scores + jnp.concatenate([mask, mask], axis=0)
-            peak = jnp.max(scores, axis=-1, keepdims=True)
-            expo = jnp.exp2((scores - peak) * (head**-0.5 * np.log2(np.e)))
-            mixed = jnp.dot(
-                expo.astype(jnp.bfloat16), value_buf[:high], preferred_element_type=jnp.float32
-            )
-            result = (mixed[:, :head] / mixed[:, head:]).astype(jnp.bfloat16)
-            for half in range(2):
-                at = pl.multiple_of((c - 1) * (2 * head) + half * head, head)
-                out_ref[low:high, pl.ds(at, head)] = result[half * rows : (half + 1) * rows]
+        scores = lax.dot_general(
+            jnp.concatenate(query, axis=0),
+            key_buf[...],
+            (((1,), (1,)), ((), ())),
+            preferred_element_type=jnp.float32,
+        )
+        scores = scores + jnp.concatenate([mask_buf[...], mask_buf[...]], axis=0)
+        peak = jnp.max(scores, axis=-1, keepdims=True)
+        expo = jnp.exp2((scores - peak) * (head**-0.5 * np.log2(np.e)))
+        total = jnp.sum(expo, axis=-1, keepdims=True)
+        mixed = jnp.dot(
+            expo.astype(jnp.bfloat16), value_buf[...], preferred_element_type=jnp.float32
+        )
+        result = (mixed / total).astype(jnp.bfloat16)
+        for half in range(2):
+            at = pl.multiple_of((c - 1) * (2 * head) + half * head, head)
+            out_ref[:, pl.ds(at, head)] = result[half * capacity : (half + 1) * capacity]
 
     def wait_last(c):
         for half in range(2):
@@ -419,7 +415,7 @@
             pltpu.VMEM((total_tokens, 2 * HEAD_SIZE), jnp.float32),
             pltpu.VMEM((total_tokens, 2 * HEAD_SIZE), bf16),
             pltpu.VMEM((capacity, HEAD_SIZE), bf16),
-            pltpu.VMEM((capacity, 2 * HEAD_SIZE), bf16),
+            pltpu.VMEM((capacity, HEAD_SIZE), bf16),
             pltpu.VMEM((capacity, HEAD_SIZE), jnp.float32),
             pltpu.VMEM((capacity, HEAD_SIZE), jnp.float32),
             pltpu.VMEM((capacity, HEAD_SIZE), jnp.int32),
@@ -443,7 +439,8 @@
 
 def body(tokens, wq, wk, wv, doc_len, doc_shard, doc_slot):
     shards = lax.axis_size("ctx")
-    if wk.shape[1] == HEAD_SIZE and shards & (shards - 1) == 0:
+    paired = wq.shape[1] % (2 * HEAD_SIZE) == 0
+    if wk.shape[1] == HEAD_SIZE and shards & (shards - 1) == 0 and paired:
         return fused(tokens, wq, wk, wv, doc_len, doc_shard, doc_slot)
     return plain(tokens, wq, wk, wv, doc_len, doc_shard, doc_slot)
 

time: 42 us -> 41.4 us (0.986)
  Pallas kernels: 40.9 us -> 40.4 us
    pallas_call x1, Pallas kernels: 40.9 us -> 40.4 us  [fused(): pl.pallas_call(functools.partial(fused_kernel, shards, capacity, heads_he...]
where the time goes in v6:
time: 41.4 us; the launch traced here: 41.3 us
  Pallas kernels  40.4 us (98%)
  local copies, waits for them, and re-layouts  0.88 us (2%)
    pallas_call x1, Pallas kernels, fused(): pl.pallas_call(functools.partial(fused_kernel, shards, capacity, heads_he...  40.4 us
    unnamed x1, local copies, waits for them, and re-layouts  0.88 us

profile of v6, /device:TPU:0, one launch (start us, length us, event | category | flops | bytes accessed | tf_op | source)
XLA Modules:
  0.0 41.3 jit_solution(8891063309715338850)
XLA Ops:
  0.0 40.4 %shard_map.82 = bf16[192,2048]{1,0:T(8,128)(2,1)S(1)} custom-call(s32[16]{0:T(128)} %len_hbm.1, s32[16]{0:T(128)} %shard_hbm.1, s32[16]{0:T(128)} %slot_hbm.1, f32[1,128]{1,0:T(1,128)} %constant.2.clone.freq_hbm, bf16[512,4096]{1,0:T(8,128)(2,1)} %tokens_hbm.1, bf16[4096,2048]{1,0:T(8,128)(2,1)} %wq_hbm.1, bf16[4096,128]{1,0:T(8,128)(2,1)} %wk_hbm.1, ...), custom_call_target="tpu_custom_call" | custom-call | flops 9663676416 | bytes 23068672 | tf_op jit(solution)/shard_map/pallas_call | solution.py:400
  40.4 0.9 %copy.10 = bf16[192,2048]{1,0:T(8,128)(2,1)} copy(bf16[192,2048]{1,0:T(8,128)(2,1)S(1)} %shard_map.82) | data formatting | bytes 1572864

commit v7 on v6

--- a/solution.py
+++ b/solution.py
@@ -137,7 +137,7 @@
     piece = depth // pieces
     documents = len_ref.shape[0]
     head = HEAD_SIZE
-    lags = [2 * p for p in range(bits + 1)]
+    lags = [2 * p - 1 for p in range(bits + 1)]
     last_lag = lags[bits]
     me = lax.axis_index("ctx")
     column = lax.axis_index("tp")

time: 41.4 us -> 43.8 us (1.058)
  Pallas kernels: 40.4 us -> 42.7 us
    pallas_call x1, Pallas kernels: 40.4 us -> 42.7 us  [fused(): pl.pallas_call(functools.partial(fused_kernel, shards, capacity, heads_he...]
where the time goes in v7:
time: 43.8 us; the launch traced here: 43.6 us
  Pallas kernels  42.7 us (97%)
  local copies, waits for them, and re-layouts  0.88 us (2%)
    pallas_call x1, Pallas kernels, fused(): pl.pallas_call(functools.partial(fused_kernel, shards, capacity, heads_he...  42.7 us
    unnamed x1, local copies, waits for them, and re-layouts  0.88 us

profile of v7, /device:TPU:0, one launch (start us, length us, event | category | flops | bytes accessed | tf_op | source)
XLA Modules:
  0.0 43.6 jit_solution(4868191144756319760)
XLA Ops:
  0.0 42.7 %shard_map.82 = bf16[192,2048]{1,0:T(8,128)(2,1)S(1)} custom-call(s32[16]{0:T(128)} %len_hbm.1, s32[16]{0:T(128)} %shard_hbm.1, s32[16]{0:T(128)} %slot_hbm.1, f32[1,128]{1,0:T(1,128)} %constant.2.clone.freq_hbm, bf16[512,4096]{1,0:T(8,128)(2,1)} %tokens_hbm.1, bf16[4096,2048]{1,0:T(8,128)(2,1)} %wq_hbm.1, bf16[4096,128]{1,0:T(8,128)(2,1)} %wk_hbm.1, ...), custom_call_target="tpu_custom_call" | custom-call | flops 9663676416 | bytes 23068672 | tf_op jit(solution)/shard_map/pallas_call | solution.py:400
  42.7 0.9 %copy.10 = bf16[192,2048]{1,0:T(8,128)(2,1)} copy(bf16[192,2048]{1,0:T(8,128)(2,1)S(1)} %shard_map.82) | data formatting | bytes 1572864
